TPU v7x, 32 devices: a whole 2x2x4 slice. The times are simulated.
32 devices in a mesh: dp: 8 (over y, x, core), seq: 4 (over z).
Axes of the slice: x: 2, y: 2, z: 4, core: 2. Of those that a mesh axis runs over, the one named last changes fastest.
Arguments:
- audio: float32 [8, 163840], P(None, ('dp', 'seq')), may hold values from -0.4 to 0.4
- starts: int32 [8], replicated, may hold values from 0 to 81919, as said below
- lengths: int32 [8], replicated, may hold values from 40960 to 163840, as said below
- slots: int32 [8], replicated, may hold values from 0 to 7, each once
- conv1_weight: bfloat16 [9, 256], replicated, may hold values from -2 to 2
- conv2_weight: bfloat16 [2304, 256], replicated, may hold values from -0.125 to 0.125
- proj_weight: bfloat16 [5120, 1024], P('dp'), may hold values from -0.078125 to 0.078125
- qkv_weight: bfloat16 [1024, 3072], P('dp'), may hold values from -8 to 8
- out_weight: bfloat16 [1024, 1024], P(None, 'dp'), may hold values from -0.1875 to 0.1875
Outputs:
- regrouped: bfloat16 [8, 8, 4, 8, 1024], P('dp', None, 'seq')
- attended: bfloat16 [8, 8, 4, 8, 1024], P('dp', None, 'seq')
Inputs may be any that keep to these rules, and one draw needn't show every extreme that they name: starts plus lengths is at most 163840 for every stream; some stream's utterance covers the whole stream, and some other stream's utterance starts at 81919. `lengths`: some stream's utterance has exactly 40960 samples. `slots`: every row number appears once.
All inputs are finite; a program needn't handle non-finite values.
Results may differ from a plain program's by a relative error of at most 0.013.
Values may be sent and summed in bfloat16 or wider, within the bound.
No kernel may reach another device: no remote copies, remote signals or barrier semaphores. Data moves between devices by JAX's collectives and lax.ppermute only.
A program may use at most 128 MiB of HBM per device.

v0:
```python
import math

import jax
import jax.numpy as jnp
import numpy as np
from jax import lax
from jax.sharding import PartitionSpec as P

D = 1024
HEADS = 8
HEAD_DIM = 128
MELS = 80
N_FFT = 512
HOP = 160
W = 8


SAMPLE_RATE = 16000.0
EPS_LOG = 1e-06
EPS_NORM = 1e-05
MASKED = -1e30


def passed_along(block, axis, distance):
    devices = range(lax.axis_size(axis))
    route = [(i - distance, i) for i in devices if i - distance in devices]
    return lax.ppermute(block, axis, route)


def mel_table(size, bands):
    count = size // 2 + 1
    highest = 2595.0 * math.log10(1.0 + SAMPLE_RATE / 1400.0)
    points = np.linspace(0.0, highest, bands + 2)
    edges = 700.0 * (10.0 ** (points / 2595.0) - 1.0)
    edges[0] = 0.0
    edges[-1] = SAMPLE_RATE / 2.0
    frequency = np.arange(count) * (SAMPLE_RATE / size)
    lower = edges[:-2][None, :]
    middle = edges[1:-1][None, :]
    upper = edges[2:][None, :]
    rising = (frequency[:, None] - lower) / (middle - lower)
    falling = (upper - frequency[:, None]) / (upper - middle)
    return np.maximum(0.0, np.minimum(rising, falling)).astype(np.float32)


def spectrum_table(size):
    sample_index = jnp.arange(size, dtype=jnp.int32)
    bin_index = jnp.arange(size // 2, dtype=jnp.int32)
    phase = sample_index[:, None] * bin_index[None, :] % size
    angle = phase.astype(jnp.float32) * (2.0 * math.pi / size)
    window = 0.5 - 0.5 * jnp.cos(sample_index.astype(jnp.float32) * (2.0 * math.pi / size))
    return jnp.concatenate([jnp.cos(angle), jnp.sin(angle)], axis=1) * window[:, None]


def mel_features(extended):
    streams = extended.shape[0]
    frame_count = 4 * W + 3
    needed = (frame_count + 3) * HOP
    extended = jnp.pad(extended, ((0, 0), (0, needed - extended.shape[1])))
    hop_rows = extended.reshape(streams, frame_count + 3, HOP)
    frames = jnp.concatenate(
        [hop_rows[:, offset : offset + frame_count] for offset in range(4)], axis=2
    )
    frames = frames[:, :, :N_FFT].reshape(streams * frame_count, N_FFT)
    spectrum = jnp.dot(frames, spectrum_table(N_FFT), precision=lax.Precision.HIGHEST)
    half = N_FFT // 2
    power = spectrum[:, :half] * spectrum[:, :half] + spectrum[:, half:] * spectrum[:, half:]
    filters = jnp.asarray(mel_table(N_FFT, MELS)[:half])
    mel_power = jnp.dot(power, filters, precision=lax.Precision.HIGHEST)
    return jnp.log(mel_power + EPS_LOG).astype(jnp.bfloat16).reshape(streams, frame_count, MELS)


def first_conv(log_mel, weight):
    padded = jnp.pad(log_mel, ((0, 0), (0, 0), (1, 1)))
    outputs = (log_mel.shape[1] - 1) // 2
    width = log_mel.shape[2]
    tap_list = [
        padded[:, row_tap : row_tap + 2 * outputs - 1 : 2, col_tap : col_tap + width - 1 : 2]
        for row_tap in range(3)
        for col_tap in range(3)
    ]
    patches = jnp.stack(tap_list, axis=-1)
    result = jnp.dot(patches.reshape(-1, 9), weight, preferred_element_type=jnp.float32)
    result = jax.nn.relu(result).astype(jnp.bfloat16)
    return result.reshape(log_mel.shape[0], outputs, width // 2, weight.shape[1])


def second_conv(first, weight):
    streams, count, width, channels = first.shape
    outputs = (count - 1) // 2
    bands = width // 2
    padded = jnp.pad(first, ((0, 0), (0, 1), (1, 1), (0, 0)))
    paired = padded.reshape(streams, outputs + 1, 2, bands + 1, 2, channels)
    total = jnp.zeros((streams * outputs * bands, weight.shape[1]), jnp.float32)
    for row_tap in range(3):
        for col_tap in range(3):
            tap = paired[
                :,
                row_tap // 2 : row_tap // 2 + outputs,
                row_tap % 2,
                col_tap // 2 : col_tap // 2 + bands,
                col_tap % 2,
                :,
            ]
            index = 3 * row_tap + col_tap
            total = total + jnp.dot(
                tap.reshape(-1, channels),
                weight[index * channels : (index + 1) * channels],
                preferred_element_type=jnp.float32,
            )
    result = jax.nn.relu(total).astype(jnp.bfloat16)
    return result.reshape(streams * outputs, bands * weight.shape[1])


def layer_norm(rows):
    values = rows.astype(jnp.float32)
    mean = jnp.mean(values, axis=-1, keepdims=True)
    centered = values - mean
    variance = jnp.mean(centered * centered, axis=-1, keepdims=True)
    return (centered * lax.rsqrt(variance + EPS_NORM)).astype(jnp.bfloat16)


def frame_mask(begin, span, owners, group, blocks):
    block = jnp.arange(blocks, dtype=jnp.int32)
    offset = jnp.arange(W, dtype=jnp.int32)
    frame = (block[None, :, None] * group + owners[:, None, None]) * W + offset[None, None, :]
    sample = frame * (4 * HOP)
    return ((sample >= begin) & (sample < begin + span)).reshape(-1)


def on_device(
    audio, starts, lengths, slots, conv1_weight, conv2_weight, proj_weight, qkv_weight, out_weight
):
    streams = audio.shape[0]
    rim_width = N_FFT + 2 * HOP
    rim_audio = passed_along(audio[:, audio.shape[1] - rim_width :], ("dp", "seq"), 1)
    log_mel = mel_features(jnp.concatenate([rim_audio, audio], axis=1))
    first = first_conv(log_mel, conv1_weight)
    features = second_conv(first, conv2_weight)
    projected = jnp.dot(
        features,
        lax.all_gather(proj_weight, "dp", axis=0, tiled=True),
        preferred_element_type=jnp.float32,
    ).astype(jnp.bfloat16)
    routing = (slots[None, :] == jnp.arange(streams, dtype=jnp.int32)[:, None]).astype(jnp.bfloat16)
    ordered = jnp.dot(
        routing, projected.reshape(streams, W * D), preferred_element_type=jnp.float32
    )
    ordered = ordered.astype(jnp.bfloat16).reshape(streams, W, D)
    received = lax.all_to_all(ordered, "dp", split_axis=0, concat_axis=0, tiled=True)
    rows_here = received.reshape(streams * W, D)
    local_count = rows_here.shape[0]
    mine = lax.axis_index("dp")
    group = lax.axis_size("seq")
    owner = lax.axis_index("seq")
    chosen = slots == mine
    begin = jnp.sum(jnp.where(chosen, starts, 0))
    span = jnp.sum(jnp.where(chosen, lengths, 0))
    valid = frame_mask(begin, span, jnp.reshape(owner, (1,)), group, streams)
    normed = layer_norm(rows_here)
    scale = HEAD_DIM ** (-0.5)
    share = HEADS // group
    head_start = owner * share
    local_rows = qkv_weight.shape[0]
    per_head = qkv_weight.reshape(local_rows, 3, HEADS, HEAD_DIM)
    mine_mix = lax.dynamic_slice_in_dim(per_head, head_start, share, 2).reshape(
        local_rows, 3 * share * HEAD_DIM
    )
    mine_out = lax.dynamic_slice_in_dim(out_weight, head_start * HEAD_DIM, share * HEAD_DIM, 0)
    weights_mix, weights_out = (
        lax.all_gather(mine_mix, "dp", axis=0, tiled=True),
        lax.all_gather(mine_out, "dp", axis=1, tiled=True),
    )
    everyone = lax.all_gather(normed, "seq", axis=0, tiled=True)
    mixed = jnp.dot(everyone, weights_mix, preferred_element_type=jnp.float32).astype(jnp.bfloat16)
    width = share * HEAD_DIM
    queries = mixed[:, :width].reshape(-1, share, HEAD_DIM)
    keys_all = mixed[:, width : 2 * width].reshape(-1, share, HEAD_DIM)
    values_all = mixed[:, 2 * width :].reshape(-1, share, HEAD_DIM)
    key_valid = frame_mask(begin, span, jnp.arange(group, dtype=jnp.int32), group, streams)
    scores = (
        jnp.einsum("qhd,khd->hqk", queries, keys_all, preferred_element_type=jnp.float32) * scale
    )
    masked = jnp.where(key_valid[None, None, :], scores, MASKED)
    peak = jnp.max(masked, axis=2, keepdims=True)
    weights = jnp.where(key_valid[None, None, :], jnp.exp(masked - peak), 0.0)
    total = jnp.sum(weights, axis=2)
    summed = jnp.einsum(
        "hqk,khd->qhd", weights.astype(jnp.bfloat16), values_all, preferred_element_type=jnp.float32
    )
    context = (
        (summed / total.T[:, :, None])
        .reshape(local_count * lax.axis_size("seq"), width)
        .astype(jnp.bfloat16)
    )
    output = lax.psum_scatter(
        jnp.dot(context, weights_out, preferred_element_type=jnp.float32).astype(jnp.bfloat16),
        "seq",
        scatter_dimension=0,
        tiled=True,
    ).astype(jnp.float32)
    regrouped = jnp.where(valid[:, None], rows_here, jnp.zeros_like(rows_here)).reshape(
        1, streams, 1, W, D
    )
    attended = (
        jnp.where(valid[:, None], output, 0.0).astype(jnp.bfloat16).reshape(1, streams, 1, W, D)
    )
    return (regrouped, attended)


def solution(mesh):
    in_specs = (
        P(None, ("dp", "seq")),
        P(),
        P(),
        P(),
        P(),
        P(),
        P("dp", None),
        P("dp", None),
        P(None, "dp"),
    )
    out_specs = (P("dp", None, "seq", None, None), P("dp", None, "seq", None, None))
    return jax.shard_map(
        on_device, mesh=mesh, in_specs=in_specs, out_specs=out_specs, check_vma=False
    )
```

profile of v0, /device:TPU:0, one launch (start us, length us, event | category | flops | bytes accessed | tf_op | source)
XLA Modules:
  0.0 148.0 jit_solution(9684273216136049957)
XLA Ops:
  8.2 4.9 %collective-permute-start = (f32[8,832]{1,0:T(8,128)S(1)}, f32[8,832]{1,0:T(8,128)S(1)}, u32[]{:S(2)}, u32[]{:S(2)}) collective-permute-start(f32[8,832]{1,0:T(8,128)S(1)} %slice.116), channel_id=1, source_target_pairs={{0,1},{1,2},{2,3},{3,4},{4,5},{5,6},{6,7},{7,8},{8,9},{9,10},{10,1... | collective-permute-start | bytes 79880 | tf_op jit(solution)/shard_map/ppermute | solution.py:27
  13.6 0.8 reshape.225
  14.4 2.1 %fusion.30 = (f32[512,256]{1,0:T(8,128)S(1)}, f32[512,256]{1,0:T(8,128)S(1)}) fusion(), kind=kLoop, calls=%fused_computation.58 | loop fusion | flops 1835008 | bytes 1048576 | tf_op jit(solution)/shard_map/sin | solution.py:52
  20.2 1.3 fusion.12
  22.9 0.7 slice.125
  23.7 0.7 slice.126
  25.1 0.7 slice.128
  25.9 0.7 slice.129
  26.6 0.7 slice.130
  27.4 0.7 slice.131
  28.1 0.7 slice.132
  30.5 0.9 fusion.1
  31.4 0.7 copy.19
  32.3 1.8 %fusion.65 = (bf16[8,8,1,20,1,256]{5,0,4,3,2,1:T(8,128)(2,1)S(1)}, bf16[8,8,1,20,1,256]{5,0,4,3,2,1:T(8,128)(2,1)}, bf16[8,8,1,20,1,256]{5,0,4,3,2,1:T(8,128)(2,...) fusion(bf16[8,9,2,21,2,256]{5,0,4,3,2,1:T(8,128)(2,1)S(1)} %bit, ...), kind=kLoop, calls=%fused_computation.108 | loop fusion | bytes 11796480 | tf_op jit(solution)/shard_map/slice | solution.py:97
  34.3 1.0 reshape_squeeze.27
  35.3 1.2 copy.21
  36.6 0.9 reshape_squeeze.28
  37.5 1.2 copy.22
  38.7 1.0 reshape_squeeze.29
  39.7 1.2 copy.23
  41.0 1.0 reshape_squeeze.30
  41.9 1.2 copy.24
  43.2 1.0 reshape_squeeze.31
  44.3 1.0 reshape_squeeze.32
  45.4 1.0 reshape_squeeze.33
  46.4 1.4 fusion.45
  48.3 0.7 copy-done.4
  49.4 0.8 copy-done.5
  50.4 0.8 copy-done.6
  51.5 0.8 copy-done.7
  52.6 0.7 copy-done.8
  53.7 0.9 copy-done.1
  54.7 1.0 reshape_squeeze.34
  55.9 1.0 reshape_squeeze.35
  57.1 1.3 convolution_add_fusion.1
  58.4 1.2 fusion.3
  59.6 0.7 reshape.221
  60.4 15.6 %all-gather.3.cloned.1.call-done = bf16[5120,1024]{1,0:T(8,128)(2,1)} async-done(((bf16[640,1024]{1,0:T(8,128)(2,1)}), bf16[5120,1024]{1,0:T(8,128)(2,1)}) %all-gather.3.cloned.1.call-update) | async-done | bytes 10485776 | tf_op jit(solution)/shard_map/all_gather | solution.py:142
  75.9 5.9 %convolution_convert_fusion.3 = bf16[64,1024]{1,0:T(8,128)(2,1)S(1)} fusion(bf16[64,5120]{1,0:T(8,128)(2,1)S(1)} %reshape.221, bf16[5120,1024]{1,0:T(8,128)(2,1)} %all-gather.3.cloned.1.call-done), kind=kOutput, calls=%fused_computation.24 | convolution fusion | flops 671154176 | bytes 11272192 | tf_op jit(solution)/shard_map/dot_general | solution.py:140
  82.1 0.7 copy.29
  82.8 3.4 %all-to-all-start = ((bf16[8,8,1024]{2,1,0:T(8,128)(2,1)}), bf16[8,8,1024]{2,1,0:T(8,128)(2,1)S(1)}, u32[]{:S(2)}, u32[]{:S(2)}) async-start(bf16[8,8,1024]{2,1,0:T(8,128)(2,1)} %copy.29), calls=%async_computation | async-start | bytes 262144 | tf_op jit(solution)/shard_map/all_to_all | solution.py:150
  86.2 10.7 %all_gather.15 = bf16[256,1024]{1,0:T(8,128)(2,1)S(1)} all-gather(bf16[256,128]{1,0:T(8,128)(2,1)S(1)} %constant_dynamic-slice_fusion), channel_id=1, replica_groups=mesh['dp'=8,'seq'=4] {'dp'}, dimensions={1}, use_global_device_ids=true | all-gather | bytes 589824 | tf_op jit(solution)/shard_map/all_gather | solution.py:172
  97.5 16.1 %all_gather.13 = bf16[256,1024]{1,0:T(8,128)(2,1)S(1)} all-gather(bf16[64,1024]{1,0:T(8,128)(2,1)S(1)} %fusion.26), channel_id=1, replica_groups=mesh['dp'=8,'seq'=4] {'seq'}, dimensions={0}, use_global_device_ids=true | all-gather | bytes 655360 | tf_op jit(solution)/shard_map/all_gather | solution.py:174
  113.6 2.0 %convolution_convert_fusion.2 = bf16[256,768]{1,0:T(8,128)(2,1)S(1)} fusion(bf16[256,1024]{1,0:T(8,128)(2,1)S(1)} %all_gather.13, bf16[1024,768]{1,0:T(8,128)(2,1)} %all-gather.5.cloned.1.call-done), kind=kOutput, calls=%fused_computation.16 | convolution fusion | flops 402849792 | bytes 2490368 | tf_op jit(solution)/shard_map/dot_general | solution.py:175
  116.6 1.1 convolution_convert_fusion.1
  119.3 0.7 select_bitcast_fusion
  120.1 19.7 %reduce-scatter.2.cloned.1.call-done = bf16[64,1024]{1,0:T(8,128)(2,1)} async-done(((bf16[256,1024]{1,0:T(8,128)(2,1)}), bf16[64,1024]{1,0:T(8,128)(2,1)}) %reduce-scatter.2.cloned.1.call-update) | async-done | bytes 131088 | tf_op jit(solution)/shard_map/reduce_scatter | solution.py:196
  139.8 1.6 %fusion.32 = bf16[1,8,1,8,1024]{4,3,2,1,0:T(8,128)(2,1)} fusion(bf16[64,1024]{1,0:T(8,128)(2,1)} %reduce-scatter.2.cloned.1.call-done, pred[64]{0:T(512)(128)(4,1)S(1)} %compare_and_fusion), kind=kLoop, calls=%fused_computation.62 | loop fusion | flops 196608 | bytes 262208
  (104 shorter events, 14.1 us)
Async XLA Ops:
  7.2 12.0 %copy-start = (bf16[1024,128]{1,0:T(8,128)(2,1)S(1)}, bf16[1024,128]{1,0:T(8,128)(2,1)}, u32[]{:S(2)}) copy-start(bf16[1024,128]{1,0:T(8,128)(2,1)} %param.18) | copy-start | bytes 786436
  7.2 1.0 copy-start.13
  7.2 6.0 %copy-start.12 = (bf16[128,3072]{1,0:T(8,128)(2,1)S(1)}, bf16[128,3072]{1,0:T(8,128)(2,1)}, u32[]{:S(2)}) copy-start(bf16[128,3072]{1,0:T(8,128)(2,1)} %param.17) | copy-start | bytes 2359300
  7.2 68.7 %all-gather.3.cloned.1.call-start = ((), (), s32[]{:S(2)}) async-start(), calls=%async_computation.2 | async-start | bytes 11796480 | tf_op jit(solution)/shard_map/all_gather | solution.py:142
  7.9 105.6 %all-gather.5.cloned.1.call-start = ((), (), s32[]{:S(2)}) async-start(), calls=%async_computation.3 | async-start | bytes 1769472 | tf_op jit(solution)/shard_map/all_gather | solution.py:171
  8.2 11.1 %collective-permute-start = (f32[8,832]{1,0:T(8,128)S(1)}, f32[8,832]{1,0:T(8,128)S(1)}, u32[]{:S(2)}, u32[]{:S(2)}) collective-permute-start(f32[8,832]{1,0:T(8,128)S(1)} %slice.116), channel_id=1, source_target_pairs={{0,1},{1,2},{2,3},{3,4},{4,5},{5,6},{6,7},{7,8},{8,9},{9,10},{10,1... | collective-permute-start | bytes 79880 | tf_op jit(solution)/shard_map/ppermute | solution.py:27
  13.3 3.1 %copy-start.16 = (s32[8]{0:T(128)S(1)}, s32[8]{0:T(128)}, u32[]{:S(2)}) copy-start(s32[8]{0:T(128)} %param.13) | copy-start | bytes 100
  13.3 3.1 %copy-start.17 = (s32[8]{0:T(128)S(1)}, s32[8]{0:T(128)}, u32[]{:S(2)}) copy-start(s32[8]{0:T(128)} %param.12) | copy-start | bytes 100
  13.3 3.1 %copy-start.18 = (s32[8]{0:T(128)S(1)}, s32[8]{0:T(128)}, u32[]{:S(2)}) copy-start(s32[8]{0:T(128)} %param.11) | copy-start | bytes 100
  20.2 1.3 copy-start.14
  21.4 9.0 %copy-start.15 = (bf16[9,256]{1,0:T(8,128)(2,1)S(1)}, bf16[9,256]{1,0:T(8,128)(2,1)}, u32[]{:S(2)}) copy-start(bf16[9,256]{1,0:T(8,128)(2,1)} %param.14) | copy-start | bytes 13828
  45.3 1.1 copy-start.2
  46.4 1.4 copy-start.3
  46.4 1.5 %copy-start.11 = (bf16[2304,256]{1,0:T(8,128)(2,1)S(1)}, bf16[2304,256]{1,0:T(8,128)(2,1)}, u32[]{:S(2)}) copy-start(bf16[2304,256]{1,0:T(8,128)(2,1)} %param.15) | copy-start | bytes 3538948
  47.9 1.1 copy-start.4
  49.0 1.1 copy-start.5
  50.1 1.1 copy-start.6
  51.2 1.1 copy-start.7
  52.3 1.1 copy-start.8
  53.4 1.2 copy-start.1
  55.9 1.2 copy-start.9
  57.1 1.3 copy-start.10
  82.8 14.1 %all-to-all-start = ((bf16[8,8,1024]{2,1,0:T(8,128)(2,1)}), bf16[8,8,1024]{2,1,0:T(8,128)(2,1)S(1)}, u32[]{:S(2)}, u32[]{:S(2)}) async-start(bf16[8,8,1024]{2,1,0:T(8,128)(2,1)} %copy.29), calls=%async_computation | async-start | bytes 262144 | tf_op jit(solution)/shard_map/all_to_all | solution.py:150
  86.2 53.6 %reduce-scatter.2.cloned.1.call-start = ((), (), s32[]{:S(2)}) async-start(), calls=%async_computation.4 | async-start | bytes 655360 | tf_op jit(solution)/shard_map/reduce_scatter | solution.py:196
Sparse Core Ops, SparseCore 0:
  9.9 65.9 all-gather.2
  77.8 27.4 all-gather.4
  117.8 21.8 reduce-scatter.1
where the time goes:
time: 149 us; the launch traced here: 148 us
  waiting for transfers between devices  36 us (24%)
  local copies, waits for them, and re-layouts  34.5 us (23%)
  blocking collectives  26.8 us (18%)
  matrix products  18.5 us (12%)
  between operations  15.7 us (11%)
  starting transfers between devices  8.41 us (6%)
  other arithmetic  8.07 us (5%)
    reduce_scatter x1, waiting for transfers between devices, on_device(): lax.psum_scatter(jnp.dot(context, weights_out, preferred_element_type=jnp...  19.7 us
    all_gather x1, blocking collectives, on_device(): everyone = lax.all_gather(normed, 'seq', axis=0, tiled=True)  16.1 us
    all_gather x1, waiting for transfers between devices, on_device(): lax.all_gather(proj_weight, 'dp', axis=0, tiled=True)  15.6 us
    all_gather x1, blocking collectives, on_device(): lax.all_gather(mine_out, 'dp', axis=1, tiled=True)  10.7 us
    another operation x9, local copies, waits for them, and re-layouts, second_conv(): tap.reshape(-1, channels)  8.9 us
    slice x10, local copies, waits for them, and re-layouts, second_conv(): paired[:, row_tap // 2:row_tap // 2 + outputs, row_tap % 2, col_tap // 2:...  7.41 us
    slice x9, local copies, waits for them, and re-layouts, first_conv(): padded[:, row_tap:row_tap + 2 * outputs - 1:2, col_tap:col_tap + width -...  6.64 us
    dot_general x1, matrix products, on_device(): jnp.dot(features, lax.all_gather(proj_weight, 'dp', axis=0, tiled=True),...  5.91 us
  transfers between devices with their start and end apart: 5, of which 2 were waited for; matrix products, arithmetic and copies ran while one was open for 34% of the time, Pallas kernels for 0%

commit v1 on v0

v1 whole, which is shorter than its diff:
```python
import functools
import math

import jax
import jax.numpy as jnp
import numpy as np
from jax import lax
from jax.experimental import pallas as pl
from jax.experimental.pallas import tpu as pltpu
from jax.sharding import PartitionSpec as P

HEADS = 8
HEAD_DIM = 128
MELS = 80
BANDS = MELS // 4
N_FFT = 512
HOP = 160
W = 8
RIM = 1024
SPAN = 4 * HOP
JS = W + 1
LANES = 128
SAMPLE_RATE = 16000.0
EPS_LOG = 1e-06
EPS_NORM = 1e-05
MASKED = -1e30
F32 = jnp.float32
BF16 = jnp.bfloat16
MIB = 1 << 20


def mel_table(size, bands):
    count = size // 2 + 1
    highest = 2595.0 * math.log10(1.0 + SAMPLE_RATE / 1400.0)
    points = np.linspace(0.0, highest, bands + 2)
    edges = 700.0 * (10.0 ** (points / 2595.0) - 1.0)
    edges[0] = 0.0
    edges[-1] = SAMPLE_RATE / 2.0
    frequency = np.arange(count) * (SAMPLE_RATE / size)
    lower = edges[:-2][None, :]
    middle = edges[1:-1][None, :]
    upper = edges[2:][None, :]
    rising = (frequency[:, None] - lower) / (middle - lower)
    falling = (upper - frequency[:, None]) / (upper - middle)
    return np.maximum(0.0, np.minimum(rising, falling)).astype(np.float32)


def filter_table():
    table = mel_table(N_FFT, MELS)[: N_FFT // 2]
    return np.pad(table, ((0, 0), (0, LANES - MELS)))


def spectrum_table(size):
    sample = np.arange(size)
    phase = sample[:, None] * np.arange(size // 2)[None, :] % size
    angle = phase * (2.0 * math.pi / size)
    window = 0.5 - 0.5 * np.cos(sample * (2.0 * math.pi / size))
    both = np.concatenate([np.cos(angle), np.sin(angle)], axis=1) * window[:, None]
    return both.astype(np.float32)


def band_selection(parts):
    share = BANDS // parts
    width = 4 * share + 4
    table = np.zeros((5 * LANES, parts * LANES), np.float32)
    for part in range(parts):
        for delta in range(5):
            for lane in range(width):
                band = 4 * share * part - 4 + lane
                if 0 <= band < MELS:
                    table[delta * LANES + band, part * LANES + delta * width + lane] = 1.0
    return table.astype(BF16)


def tap_selection(parts):
    share = BANDS // parts
    width = 4 * share + 4
    outs = 2 * share + 1
    table = np.zeros((outs, LANES, 16), np.float32)
    for g in range(outs):
        for row_tap in range(3):
            for col_tap in range(3):
                table[g, row_tap * width + 2 * g + 1 + col_tap, 3 * row_tap + col_tap] = 1.0
    return table.reshape(outs * LANES, 16).astype(BF16)


def swap_table(outer, inner):
    count = outer * inner
    table = np.zeros((count, count), np.float32)
    for o in range(outer):
        for i in range(inner):
            table[i * outer + o, o * inner + i] = 1.0
    return table.astype(BF16)


def frame_table(windows):
    count = windows * W
    table = np.zeros((count, count), np.float32)
    for k in range(windows):
        for t in range(W):
            table[k * W + t, (k // 8) * 8 * W + t * 8 + k % 8] = 1.0
    return table.astype(BF16)


def vmem():
    return pl.BlockSpec(memory_space=pltpu.VMEM)


def smem():
    return pl.BlockSpec(memory_space=pltpu.SMEM)


def anywhere():
    return pl.BlockSpec(memory_space=pl.ANY)


def params(mib):
    return pltpu.CompilerParams(vmem_limit_bytes=mib * MIB)


def cost(flops, moved):
    return pl.CostEstimate(flops=int(flops), bytes_accessed=int(moved), transcendentals=0)


def prep_kernel(
    columns, chips, width, proj_ref, qkv_ref, taps_ref, conv1_ref, proj_out, mix_out, banded_out, mix_buf, sems
):
    features = qkv_ref.shape[1] // 3
    first = pl.multiple_of(lax.axis_index("seq") * width, LANES)
    loads = [
        pltpu.make_async_copy(
            qkv_ref.at[:, pl.ds(part * features + first, width)],
            mix_buf.at[:, pl.ds(part * width, width)],
            sems.at[part],
        )
        for part in range(3)
    ]
    for copy in loads:
        copy.start()
    pieces = [
        pltpu.make_async_copy(proj_ref.at[:, pl.ds(n * columns, columns)], proj_out.at[n], sems.at[3 + n])
        for n in range(proj_out.shape[0])
    ]
    for copy in pieces:
        copy.start()
    outs = banded_out.shape[1] // conv1_ref.shape[1]
    channels = conv1_ref.shape[1]
    for copy in loads:
        copy.wait()
    base = 3 + proj_out.shape[0]
    stores = [pltpu.make_async_copy(mix_buf, mix_out.at[n], sems.at[base + n]) for n in range(chips)]
    for copy in stores:
        copy.start()
    for g in range(outs):
        banded_out[:, g * channels : (g + 1) * channels] = jnp.dot(
            taps_ref[g * LANES : (g + 1) * LANES, :], conv1_ref[...], preferred_element_type=F32
        ).astype(BF16)
    for copy in pieces + stores:
        copy.wait()


def mel_kernel(parts, rim_ref, audio_ref, table_ref, filter_ref, select_ref, slots_ref, out_ref, ext):
    streams = audio_ref.shape[0]
    rows = JS * streams
    ext[:, :RIM] = rim_ref[...]
    ext[:, RIM:] = audio_ref[...]
    phases = []
    for phase in range(4):
        start = HOP * phase + 32
        base, shift = start // LANES * LANES, start % LANES
        length = N_FFT + (LANES if shift else 0)
        block = jnp.concatenate(
            [ext[:, SPAN * j + base : SPAN * j + base + length] for j in range(JS)], axis=0
        )
        if shift:
            block = pltpu.roll(block, length - shift, 1)[:, :N_FFT]
        phases.append(block)
    frames = jnp.concatenate(phases, axis=0)
    spectrum = jnp.dot(frames, table_ref[...], precision=lax.Precision.HIGHEST, preferred_element_type=F32)
    half = N_FFT // 2
    real, imag = spectrum[:, :half], spectrum[:, half:]
    power = real * real + imag * imag
    mel_power = jnp.dot(power, filter_ref[...], precision=lax.Precision.HIGHEST, preferred_element_type=F32)
    log_mel = jnp.log(mel_power + EPS_LOG)
    by_phase = [log_mel[phase * rows : (phase + 1) * rows] for phase in range(4)]

    def later(block):
        return jnp.concatenate([block[streams:], jnp.zeros((streams, LANES), F32)], axis=0)

    taps = [by_phase[1], by_phase[2], by_phase[3], later(by_phase[0]), later(by_phase[1])]
    gathered = jnp.concatenate([tap.astype(BF16) for tap in taps], axis=1)
    placed = jnp.dot(gathered, select_ref[...], preferred_element_type=F32).astype(BF16)
    routing = (slots_ref[...] == lax.broadcasted_iota(jnp.int32, (rows, rows), 0)).astype(F32).astype(BF16)
    routed = jnp.dot(routing, placed, preferred_element_type=F32).astype(BF16)
    copies = out_ref.shape[0] // parts
    for part in range(parts):
        block = routed[:, part * LANES : (part + 1) * LANES]
        for copy in range(copies):
            out_ref[part * copies + copy] = block


def conv_kernel(
    width, mel_ref, swap_ref, banded_ref, conv2_ref, proj_ref, out_ref, even, odd, second, conv2, proj, sems
):
    streams = out_ref.shape[0]
    n = 8 * streams
    step = pl.program_id(0)
    load_conv2 = pltpu.make_async_copy(conv2_ref, conv2, sems.at[0])
    load_proj = pltpu.make_async_copy(proj_ref, proj, sems.at[1])

    @pl.when(step == 0)
    def _():
        load_conv2.start()
        load_proj.start()

    blocks = [mel_ref[d].astype(F32) for d in range(8)]
    ordered = jnp.concatenate(
        [
            jnp.concatenate([block[j * streams : (j + 1) * streams] for block in blocks], axis=0)
            for j in range(JS)
        ],
        axis=1,
    ).astype(BF16)
    swapped = jnp.dot(swap_ref[...], ordered, preferred_element_type=F32)
    by_j = [swapped[:, j * LANES : (j + 1) * LANES] for j in range(JS)]
    evens = jnp.concatenate(by_j, axis=0)
    odds = pltpu.roll(evens[: W * n], LANES - 2 * width, 1).astype(BF16)
    evens = evens.astype(BF16)
    channels = conv2_ref.shape[1]
    outs = banded_ref.shape[1] // channels
    for g in range(outs):
        lanes = slice(g * channels, (g + 1) * channels)
        weight = banded_ref[:, lanes]
        even[:, lanes] = jax.nn.relu(jnp.dot(evens, weight, preferred_element_type=F32)).astype(BF16)
        odd[:, lanes] = jax.nn.relu(jnp.dot(odds, weight, preferred_element_type=F32)).astype(BF16)

    @pl.when(step == 0)
    def _():
        load_conv2.wait()
        load_proj.wait()

    for h in range((outs - 1) // 2):
        lanes = slice(2 * h * channels, (2 * h + 3) * channels)
        depth = 3 * channels
        total = jnp.dot(even[: W * n, lanes], conv2[:depth], preferred_element_type=F32)
        total += jnp.dot(odd[:, lanes], conv2[depth : 2 * depth], preferred_element_type=F32)
        total += jnp.dot(even[n:, lanes], conv2[2 * depth :], preferred_element_type=F32)
        second[:, h * channels : (h + 1) * channels] = jax.nn.relu(total).astype(BF16)
    weights = proj[...].reshape(second.shape[1], proj.shape[2])
    partial = jnp.dot(second[...], weights, preferred_element_type=F32)
    for r in range(streams):
        out_ref[r, 0] = jnp.concatenate(
            [partial[t * n + r * 8 : t * n + r * 8 + 8] for t in range(W)], axis=0
        ).astype(BF16)


def bounds(slots_ref, starts_ref, lengths_ref):
    mine = lax.axis_index("dp")
    begin, span = jnp.int32(0), jnp.int32(0)
    for u in range(slots_ref.shape[0]):
        chosen = slots_ref[u] == mine
        begin = begin + jnp.where(chosen, starts_ref[u], 0)
        span = span + jnp.where(chosen, lengths_ref[u], 0)
    return begin, begin + span


def norm_kernel(parts, slots_ref, starts_ref, lengths_ref, part_ref, frames_ref, sample_ref, rows_out, normed_out):
    begin, end = bounds(slots_ref, starts_ref, lengths_ref)
    copies = part_ref.shape[0] // parts
    halves = []
    for copy in range(copies):
        total = part_ref[copy].astype(F32)
        for part in range(1, parts):
            total += part_ref[part * copies + copy].astype(F32)
        halves.append(total)
    encoded = jnp.concatenate(halves, axis=1).astype(BF16)
    values = jnp.dot(frames_ref[...], encoded, preferred_element_type=F32)
    sample = sample_ref[...] + lax.axis_index("seq") * (W * SPAN)
    valid = (sample >= begin) & (sample < end)
    rows_out[...] = jnp.where(valid, values, 0.0).astype(BF16)
    mean = jnp.mean(values, axis=-1, keepdims=True)
    centered = values - mean
    variance = jnp.mean(centered * centered, axis=-1, keepdims=True)
    normed = (centered * lax.rsqrt(variance + EPS_NORM)).astype(BF16)
    for copy in range(normed_out.shape[0]):
        normed_out[copy] = normed


def gathered_copies(mine_ref, other_ref, buffer, sems):
    core = lax.axis_index("dp") % 2
    copies = []
    for chip in range(mine_ref.shape[0]):
        copies.append(pltpu.make_async_copy(mine_ref.at[chip], buffer.at[2 * chip + core], sems.at[2 * chip]))
        copies.append(
            pltpu.make_async_copy(other_ref.at[chip], buffer.at[2 * chip + 1 - core], sems.at[2 * chip + 1])
        )
    return copies


def attention_kernel(
    slots_ref, starts_ref, lengths_ref, normed_ref, sample_ref, mine_ref, other_ref, out_ref, buffer, sems
):
    copies = gathered_copies(mine_ref, other_ref, buffer, sems)
    for copy in copies:
        copy.start()
    begin, end = bounds(slots_ref, starts_ref, lengths_ref)
    sample = sample_ref[...]
    valid = (sample >= begin) & (sample < end)
    group, local, features = normed_ref.shape
    normed = normed_ref[...].reshape(group * local, features)
    for copy in copies:
        copy.wait()
    weights = buffer[...].reshape(features, buffer.shape[2])
    mixed = jnp.dot(normed, weights, preferred_element_type=F32).astype(BF16)
    width = buffer.shape[2] // 3
    scale = HEAD_DIM ** (-0.5)
    for head in range(width // HEAD_DIM):
        at = head * HEAD_DIM
        query = mixed[:, at : at + HEAD_DIM]
        key = mixed[:, width + at : width + at + HEAD_DIM]
        value = mixed[:, 2 * width + at : 2 * width + at + HEAD_DIM]
        scores = lax.dot_general(query, key, (((1,), (1,)), ((), ())), preferred_element_type=F32) * scale
        masked = jnp.where(valid, scores, MASKED)
        peak = jnp.max(masked, axis=1, keepdims=True)
        weight = jnp.where(valid, jnp.exp(masked - peak), 0.0)
        total = jnp.sum(weight, axis=1, keepdims=True)
        summed = jnp.dot(weight.astype(BF16), value, preferred_element_type=F32)
        context = (summed / total).astype(BF16)
        for part in range(group):
            out_ref[part, :, at : at + HEAD_DIM] = context[part * local : (part + 1) * local]


def output_kernel(
    slots_ref, starts_ref, lengths_ref, context_ref, sample_ref, mine_ref, other_ref, out_ref, buffer, sems
):
    copies = gathered_copies(mine_ref, other_ref, buffer, sems)
    for copy in copies:
        copy.start()
    begin, end = bounds(slots_ref, starts_ref, lengths_ref)
    context = jnp.concatenate([context_ref[part] for part in range(context_ref.shape[0])], axis=1)
    sample = sample_ref[...] + lax.axis_index("seq") * (W * SPAN)
    valid = (sample >= begin) & (sample < end)
    for copy in copies:
        copy.wait()
    result = jnp.concatenate(
        [jnp.dot(context, buffer[d], preferred_element_type=F32) for d in range(buffer.shape[0])], axis=1
    )
    out_ref[...] = jnp.where(valid, result, 0.0).astype(BF16)


def on_device(
    audio, starts, lengths, slots, conv1_weight, conv2_weight, proj_weight, qkv_weight, out_weight
):
    streams = audio.shape[0]
    windows = lax.axis_size("dp")
    group = lax.axis_size("seq")
    parts = math.gcd(windows, BANDS)
    copies = windows // parts
    chips = windows // 2
    share = BANDS // parts
    width = 4 * share + 4
    channels = conv1_weight.shape[1]
    features = proj_weight.shape[1]
    columns = features // copies
    head_width = features // group
    local = windows * W
    rows = JS * streams
    n = 8 * streams

    route = [(i, i + 1) for i in range(windows * group - 1)]
    rim = lax.ppermute(audio[:, audio.shape[1] - RIM :], ("dp", "seq"), route)

    proj_parts, mix_parts, banded = pl.pallas_call(
        functools.partial(prep_kernel, columns, chips, head_width),
        out_shape=(
            jax.ShapeDtypeStruct((copies, proj_weight.shape[0], columns), BF16),
            jax.ShapeDtypeStruct((chips, qkv_weight.shape[0], 3 * head_width), BF16),
            jax.ShapeDtypeStruct((LANES, (2 * share + 1) * channels), BF16),
        ),
        in_specs=[anywhere(), anywhere(), vmem(), vmem()],
        out_specs=(anywhere(), anywhere(), vmem()),
        scratch_shapes=[
            pltpu.VMEM((qkv_weight.shape[0], 3 * head_width), BF16),
            pltpu.SemaphoreType.DMA((3 + copies + chips,)),
        ],
        compiler_params=params(16),
        cost_estimate=cost(1e8, 8e6),
        name="prep",
    )(proj_weight, qkv_weight, jnp.asarray(tap_selection(parts)), jnp.pad(conv1_weight, ((0, 7), (0, 0))))

    same_core = [list(range(core, windows, 2)) for core in range(2)]
    swap_cores = [(i, i ^ 1) for i in range(windows)]
    neighbours = [list(range(i, i + copies)) for i in range(0, windows, copies)]
    proj_here = lax.all_to_all(
        proj_parts, "dp", split_axis=0, concat_axis=0, axis_index_groups=neighbours, tiled=True
    )
    mix_mine = lax.all_to_all(
        mix_parts, "dp", split_axis=0, concat_axis=0, axis_index_groups=same_core, tiled=True
    )
    mix_other = lax.ppermute(mix_mine, "dp", swap_cores)

    targets = (jnp.arange(JS, dtype=jnp.int32)[:, None] * streams + slots[None, :]).reshape(1, rows)
    mel = pl.pallas_call(
        functools.partial(mel_kernel, parts),
        out_shape=jax.ShapeDtypeStruct((windows, rows, LANES), BF16),
        in_specs=[vmem()] * 6,
        out_specs=vmem(),
        scratch_shapes=[pltpu.VMEM((streams, RIM + audio.shape[1]), F32)],
        compiler_params=params(24),
        cost_estimate=cost(2e9, 2e6),
        name="log_mel",
    )(
        rim,
        audio,
        jnp.asarray(spectrum_table(N_FFT)),
        jnp.asarray(filter_table()),
        jnp.asarray(band_selection(parts)),
        targets,
    )
    mel = lax.all_to_all(mel, "dp", split_axis=0, concat_axis=0, tiled=True)

    partial = pl.pallas_call(
        functools.partial(conv_kernel, width),
        grid=(windows // 8,),
        out_shape=jax.ShapeDtypeStruct((streams, windows // 8, 8 * W, columns), BF16),
        in_specs=[
            pl.BlockSpec((8, rows, LANES), lambda i: (i, 0, 0)),
            vmem(),
            vmem(),
            anywhere(),
            anywhere(),
        ],
        out_specs=pl.BlockSpec((streams, 1, 8 * W, columns), lambda i: (0, i, 0, 0)),
        scratch_shapes=[
            pltpu.VMEM((JS * n, banded.shape[1]), BF16),
            pltpu.VMEM((W * n, banded.shape[1]), BF16),
            pltpu.VMEM((W * n, share * channels), BF16),
            pltpu.VMEM(conv2_weight.shape, BF16),
            pltpu.VMEM(proj_parts.shape, BF16),
            pltpu.SemaphoreType.DMA((2,)),
        ],
        compiler_params=params(56),
        cost_estimate=cost(8e9, 4e6),
        name="conv",
    )(mel, jnp.asarray(swap_table(8, streams)), banded, conv2_weight, proj_here)
    partial = lax.all_to_all(partial, "dp", split_axis=0, concat_axis=0, tiled=True)
    partial, out_here = lax.optimization_barrier((partial, out_weight))

    index = np.arange(local)
    local_sample = ((index // W) * group * W + index % W) * SPAN
    all_sample = (local_sample[None, :] + np.arange(group)[:, None] * W * SPAN).reshape(1, -1)
    local_sample = jnp.asarray(local_sample.reshape(-1, 1).astype(np.int32))
    regrouped, normed = pl.pallas_call(
        functools.partial(norm_kernel, parts),
        out_shape=(
            jax.ShapeDtypeStruct((local, features), BF16),
            jax.ShapeDtypeStruct((group, local, features), BF16),
        ),
        in_specs=[smem()] * 3 + [vmem()] * 3,
        out_specs=(vmem(), vmem()),
        compiler_params=params(24),
        cost_estimate=cost(1e8, 1e6),
        name="layer_norm",
    )(
        slots,
        starts,
        lengths,
        partial.reshape(windows, local, columns),
        jnp.asarray(frame_table(windows)),
        local_sample,
    )
    normed = lax.all_to_all(normed, "seq", split_axis=0, concat_axis=0, tiled=True)

    out_mine = lax.all_to_all(
        jnp.broadcast_to(out_here[None], (chips,) + out_here.shape),
        "dp",
        split_axis=0,
        concat_axis=0,
        axis_index_groups=same_core,
        tiled=True,
    )
    out_other = lax.ppermute(out_mine, "dp", swap_cores)

    context = pl.pallas_call(
        attention_kernel,
        out_shape=jax.ShapeDtypeStruct((group, local, head_width), BF16),
        in_specs=[smem()] * 3 + [vmem()] * 2 + [anywhere()] * 2,
        out_specs=vmem(),
        scratch_shapes=[
            pltpu.VMEM((windows, qkv_weight.shape[0], 3 * head_width), BF16),
            pltpu.SemaphoreType.DMA((windows,)),
        ],
        compiler_params=params(48),
        cost_estimate=cost(1e9, 2e6),
        name="attention",
    )(
        slots,
        starts,
        lengths,
        normed,
        jnp.asarray(all_sample.astype(np.int32)),
        mix_mine,
        mix_other,
    )
    context = lax.all_to_all(context, "seq", split_axis=0, concat_axis=0, tiled=True)

    attended = pl.pallas_call(
        output_kernel,
        out_shape=jax.ShapeDtypeStruct((local, features), BF16),
        in_specs=[smem()] * 3 + [vmem()] * 2 + [anywhere()] * 2,
        out_specs=vmem(),
        scratch_shapes=[
            pltpu.VMEM((windows,) + out_weight.shape, BF16),
            pltpu.SemaphoreType.DMA((windows,)),
        ],
        compiler_params=params(24),
        cost_estimate=cost(1e8, 3e6),
        name="output",
    )(slots, starts, lengths, context, local_sample, out_mine, out_other)
    shape = (1, windows, 1, W, features)
    return (regrouped.reshape(shape), attended.reshape(shape))


def solution(mesh):
    in_specs = (
        P(None, ("dp", "seq")),
        P(),
        P(),
        P(),
        P(),
        P(),
        P("dp", None),
        P("dp", None),
        P(None, "dp"),
    )
    out_specs = (P("dp", None, "seq", None, None), P("dp", None, "seq", None, None))
    return jax.shard_map(
        on_device, mesh=mesh, in_specs=in_specs, out_specs=out_specs, check_vma=False
    )
```

time: 149 us -> 118 us (0.79)
  local copies, waits for them, and re-layouts: 34.5 us -> 6.28 us
  Pallas kernels: 0 us -> 19.7 us
  matrix products: 18.5 us -> 0 us
  between operations: 15.7 us -> 0.86 us
  starting transfers between devices: 8.41 us -> 19.5 us
  other arithmetic: 8.07 us -> 0.08 us
  blocking collectives: 26.8 us -> 34 us
    all_to_all x1 -> x4, waiting for transfers between devices: 0.01 us -> 35.3 us  [the longest x1 13.8 us: on_device(): lax.all_to_all(normed, 'seq', split_axis=0, concat_axis=0, tiled=True)]
    all_to_all x0 -> x3, blocking collectives: none -> 34 us  [the longest x1 13.3 us: on_device(): lax.all_to_all(partial, 'dp', split_axis=0, concat_axis=0, tiled=True)]
    all_gather x2 -> x0, blocking collectives: 26.8 us -> none  [the longest x1 16.1 us: on_device(): everyone = lax.all_gather(normed, 'seq', axis=0, tiled=True)]
    reduce_scatter x1 -> x0, waiting for transfers between devices: 19.7 us -> none  [on_device(): lax.psum_scatter(jnp.dot(context, weights_out, preferred_element_type=jnp...]
    pallas_call x0 -> x6, Pallas kernels: none -> 19.7 us  [the longest x1 8.55 us: on_device(): pl.pallas_call(functools.partial(conv_kernel, width), grid=(windows // 8,...]
    dot_general x18 -> x0, matrix products: 18.2 us -> none  [the longest x1 5.91 us: on_device(): jnp.dot(features, lax.all_gather(proj_weight, 'dp', axis=0, tiled=True),...]
    all_gather x2 -> x0, waiting for transfers between devices: 15.6 us -> none  [the longest x1 15.6 us: on_device(): lax.all_gather(proj_weight, 'dp', axis=0, tiled=True)]
    slice x21 -> x1, local copies, waits for them, and re-layouts: 14.2 us -> 0.01 us  [on_device(): rim = lax.ppermute(audio[:, audio.shape[1] - RIM:], ('dp', 'seq'), route)]
  transfers between devices with their start and end apart: 5 -> 7, of which waited for: 2 -> 4; matrix products, arithmetic and copies ran while one was open for 34% -> 0% of each run, Pallas kernels for 0% -> 7%
where the time goes in v1:
time: 118 us; the launch traced here: 117 us
  waiting for transfers between devices  36.7 us (31%)
  blocking collectives  34 us (29%)
  Pallas kernels  19.7 us (17%)
  starting transfers between devices  19.5 us (17%)
  local copies, waits for them, and re-layouts  6.28 us (5%)
    all_to_all x1, waiting for transfers between devices, on_device(): lax.all_to_all(normed, 'seq', split_axis=0, concat_axis=0, tiled=True)  13.8 us
    all_to_all x1, blocking collectives, on_device(): lax.all_to_all(partial, 'dp', split_axis=0, concat_axis=0, tiled=True)  13.3 us
    all_to_all x1, blocking collectives, on_device(): mel = lax.all_to_all(mel, 'dp', split_axis=0, concat_axis=0, tiled=True)  12.3 us
    all_to_all x1, waiting for transfers between devices, on_device(): lax.all_to_all(jnp.broadcast_to(out_here[None], (chips,) + out_here.shape...  11.1 us
    all_to_all x1, waiting for transfers between devices, on_device(): lax.all_to_all(mix_parts, 'dp', split_axis=0, concat_axis=0, axis_index_g...  10.4 us
    pallas_call x1, Pallas kernels, on_device(): pl.pallas_call(functools.partial(conv_kernel, width), grid=(windows // 8,...  8.55 us
    all_to_all x1, blocking collectives, on_device(): lax.all_to_all(context, 'seq', split_axis=0, concat_axis=0, tiled=True)  8.45 us
    ppermute x1, starting transfers between devices, on_device(): rim = lax.ppermute(audio[:, audio.shape[1] - RIM:], ('dp', 'seq'), route)  4.93 us
  transfers between devices with their start and end apart: 7, of which 4 were waited for; matrix products, arithmetic and copies ran while one was open for 0% of the time, Pallas kernels for 7%

profile of v1, /device:TPU:0, one launch (start us, length us, event | category | flops | bytes accessed | tf_op | source)
XLA Modules:
  0.0 117.1 jit_solution(1333426213110682975)
XLA Ops:
  0.6 0.7 pad.4.conv1_ref
  1.3 1.3 %copy-done = bf16[640,1024]{1,0:T(8,128)(2,1)S(1)} copy-done((bf16[640,1024]{1,0:T(8,128)(2,1)S(1)}, bf16[640,1024]{1,0:T(8,128)(2,1)}, u32[]{:S(2)}) %copy-start) | copy-done | bytes 1310744
  2.7 1.1 copy-done.1
  3.8 1.0 copy-done.2
  4.8 1.5 %prep.1 = (bf16[2,640,512]{2,1,0:T(8,128)(2,1)}, bf16[4,128,768]{2,1,0:T(8,128)(2,1)}, bf16[128,2816]{1,0:T(8,128)(2,1)S(1)}) custom-call(bf16[640,1024]{1,0:T(8,128)(2,1)S(1)} %copy-done, bf16[128,3072]{1,0:T(8,128)(2,1)S(1)} %copy-done.1, bf16[1408,16]{1,0:T(8,128)(2,1)S(1)} %copy-done.2, bf16[16,256]{1,0:T(8,128)(2,1)S(1)} %pad.4.conv1_ref), custom_call_target="tpu_custom_call" | custom-call | flops 100000000 | bytes 8000000 | tf_op jit(solution)/shard_map/prep/pallas_call | solution.py:373
  6.2 0.0 copy-start.9
  6.2 0.9 copy-done.9
  7.1 0.0 copy-start.12
  7.1 3.8 %all-to-all-start.1 = ((bf16[2,640,512]{2,1,0:T(8,128)(2,1)}), bf16[2,640,512]{2,1,0:T(8,128)(2,1)S(1)}, u32[]{:S(2)}, u32[]{:S(2)}) async-start(bf16[2,640,512]{2,1,0:T(8,128)(2,1)} %get-tuple-element.10), calls=%async_computation.1 | async-start | bytes 2621440 | tf_op jit(solution)/shard_map/all_to_all | solution.py:394
  10.9 0.0 copy-done.5
  10.9 4.9 %collective-permute-start = (f32[8,1024]{1,0:T(8,128)S(1)}, f32[8,1024]{1,0:T(8,128)S(1)}, u32[]{:S(2)}, u32[]{:S(2)}) collective-permute-start(f32[8,1024]{1,0:T(8,128)S(1)} %slice.3), channel_id=1, source_target_pairs={{0,1},{1,2},{2,3},{3,4},{4,5},{5,6},{6,7},{7,8},{8,9},{9,10},{10,1... | collective-permute-start | bytes 98312 | tf_op jit(solution)/shard_map/ppermute | solution.py:371
  15.9 0.0 copy-done.6
  15.9 0.1 broadcast_add_fusion
  15.9 0.1 add.28.slots_ref
  16.0 1.4 %collective-permute-done.rim_ref = f32[8,1024]{1,0:T(8,128)S(1)} collective-permute-done((f32[8,1024]{1,0:T(8,128)S(1)}, f32[8,1024]{1,0:T(8,128)S(1)}, u32[]{:S(2)}, u32[]{:S(2)}) %collective-permute-start) | collective-permute-done | bytes 32800 | tf_op jit(solution)/shard_map/ppermute | solution.py:371
  17.4 0.0 copy-done.10
  17.4 0.0 copy-done.11
  17.4 0.0 copy-done.12
  17.4 2.1 %log_mel.1 = bf16[8,72,128]{2,1,0:T(8,128)(2,1)S(1)} custom-call(f32[8,1024]{1,0:T(8,128)S(1)} %collective-permute-done.rim_ref, f32[8,5120]{1,0:T(8,128)S(1)} %copy-done.5, f32[512,512]{1,0:T(8,128)S(1)} %copy-done.10, f32[256,128]{1,0:T(8,128)S(1)} %copy-done.12, bf16[640,512]{1,0:T(8,128)(2,1)S(1)} %copy-done.11, s32[1,72]{1,0:T(1,128)S(1)} %add.28.slots_ref), custom_call_target="tpu_custom_call" | custom-call | flops 2000000000 | bytes 2000000 | tf_op jit(solution)/shard_map/log_mel/pallas_call | solution.py:403
  19.6 0.0 all-to-all-done.1.proj_ref
  19.6 0.0 copy-start.14
  19.6 12.3 %all_to_all.35.mel_ref = bf16[8,72,128]{2,1,0:T(8,128)(2,1)} all-to-all(bf16[8,72,128]{2,1,0:T(8,128)(2,1)S(1)} %log_mel.1), channel_id=1, replica_groups=mesh['dp'=8,'seq'=4] {'dp'}, dimensions={0} | all-to-all | bytes 294912 | tf_op jit(solution)/shard_map/all_to_all | solution.py:420
  31.9 0.0 copy-done.14
  31.9 8.6 %conv.1 = bf16[8,1,64,512]{3,2,1,0:T(8,128)(2,1)} custom-call(bf16[8,72,128]{2,1,0:T(8,128)(2,1)} %all_to_all.35.mel_ref, bf16[64,64]{1,0:T(8,128)(2,1)} %constant.23.clone.swap_ref.frames_ref, bf16[128,2816]{1,0:T(8,128)(2,1)} %copy-done.9, bf16[2304,256]{1,0:T(8,128)(2,1)} %conv2_ref.1, bf16[2,640,512]{2,1,0:T(8,128)(2,1)} %copy-done.14), custom_call_target="tpu_custom_call" | custom-call | flops 8000000000 | bytes 4000000 | tf_op jit(solution)/shard_map/conv/pallas_call | solution.py:422
  40.4 0.0 copy-start.15
  40.4 13.3 %all_to_all.36 = bf16[8,1,64,512]{3,2,1,0:T(8,128)(2,1)S(1)} all-to-all(bf16[8,1,64,512]{3,2,1,0:T(8,128)(2,1)} %conv.1), channel_id=1, replica_groups=mesh['dp'=8,'seq'=4] {'dp'}, dimensions={0} | all-to-all | bytes 1048576 | tf_op jit(solution)/shard_map/all_to_all | solution.py:446
  53.7 3.5 %all-to-all-start.4 = ((bf16[4,128,768]{2,1,0:T(8,128)(2,1)}), bf16[4,128,768]{2,1,0:T(8,128)(2,1)S(1)}, u32[]{:S(2)}, u32[]{:S(2)}) async-start(bf16[4,128,768]{2,1,0:T(8,128)(2,1)} %get-tuple-element.14), calls=%async_computation.4 | async-start | bytes 1572864 | tf_op jit(solution)/shard_map/all_to_all | solution.py:397
  57.2 10.4 %all-to-all-done.4.mine_ref = bf16[4,128,768]{2,1,0:T(8,128)(2,1)S(1)} async-done(((bf16[4,128,768]{2,1,0:T(8,128)(2,1)}), bf16[4,128,768]{2,1,0:T(8,128)(2,1)S(1)}, u32[]{:S(2)}, u32[]{:S(2)}) %all-to-all-start.4) | async-done | bytes 786464 | tf_op jit(solution)/shard_map/all_to_all | solution.py:397
  67.6 0.0 copy-done.15
  67.6 1.1 broadcast_in_dim.2
  68.8 3.7 %all-to-all-start.6 = ((bf16[4,1024,128]{2,1,0:T(8,128)(2,1)}), bf16[4,1024,128]{2,1,0:T(8,128)(2,1)S(1)}, u32[]{:S(2)}, u32[]{:S(2)}) async-start(bf16[4,1024,128]{2,1,0:T(8,128)(2,1)} %broadcast_in_dim.2), calls=%async_computation.6 | async-start | bytes 2097152 | tf_op jit(solution)/shard_map/all_to_all | solution.py:474
  72.5 0.0 copy-start.13
  72.5 0.1 collective-permute-start.1
  72.6 0.0 copy-done.3
  72.6 0.0 copy-done.4
  72.6 0.0 copy-done.7
  72.6 0.0 copy-done.8
  72.6 1.8 %layer_norm.1 = (bf16[64,1024]{1,0:T(8,128)(2,1)}, bf16[4,64,1024]{2,1,0:T(8,128)(2,1)}) custom-call(s32[8]{0:T(128)S(1)} %copy-done.6, s32[8]{0:T(128)S(1)} %copy-done.7, s32[8]{0:T(128)S(1)} %copy-done.8, bf16[8,64,512]{2,1,0:T(8,128)(2,1)S(1)} %bitcast.7, bf16[64,64]{1,0:T(8,128)(2,1)S(1)} %copy-done.4, s32[64,1]{1,0:T(8,128)S(1)} %copy-done.3), custom_call_target="tpu_custom_call" | custom-call | flops 100000000 | bytes 1000000 | tf_op jit(solution)/shard_map/layer_norm/pallas_call | solution.py:453
  74.4 11.1 %all-to-all-done.6.mine_ref = bf16[4,1024,128]{2,1,0:T(8,128)(2,1)S(1)} async-done(((bf16[4,1024,128]{2,1,0:T(8,128)(2,1)}), bf16[4,1024,128]{2,1,0:T(8,128)(2,1)S(1)}, u32[]{:S(2)}, u32[]{:S(2)}) %all-to-all-start.6) | async-done | bytes 1048608 | tf_op jit(solution)/shard_map/all_to_all | solution.py:474
  85.5 3.5 %all-to-all-start.3 = ((bf16[4,64,1024]{2,1,0:T(8,128)(2,1)}), bf16[4,64,1024]{2,1,0:T(8,128)(2,1)S(1)}, u32[]{:S(2)}, u32[]{:S(2)}) async-start(bf16[4,64,1024]{2,1,0:T(8,128)(2,1)} %get-tuple-element.13), calls=%async_computation.3 | async-start | bytes 1048576 | tf_op jit(solution)/shard_map/all_to_all | solution.py:472
  89.0 0.1 collective-permute-start.2
  89.1 0.0 collective-permute-done.1.other_ref
  89.1 13.8 %all-to-all-done.3.normed_ref = bf16[4,64,1024]{2,1,0:T(8,128)(2,1)S(1)} async-done(((bf16[4,64,1024]{2,1,0:T(8,128)(2,1)}), bf16[4,64,1024]{2,1,0:T(8,128)(2,1)S(1)}, u32[]{:S(2)}, u32[]{:S(2)}) %all-to-all-start.3) | async-done | bytes 524320 | tf_op jit(solution)/shard_map/all_to_all | solution.py:472
  102.9 0.0 copy-done.13
  102.9 3.8 %attention.1 = bf16[4,64,256]{2,1,0:T(8,128)(2,1)S(1)} custom-call(s32[8]{0:T(128)S(1)} %copy-done.6, s32[8]{0:T(128)S(1)} %copy-done.7, s32[8]{0:T(128)S(1)} %copy-done.8, bf16[4,64,1024]{2,1,0:T(8,128)(2,1)S(1)} %all-to-all-done.3.normed_ref, s32[1,256]{1,0:T(1,128)S(1)} %copy-done.13, bf16[4,128,768]{2,1,0:T(8,128)(2,1)S(1)} %all-to-all-done.4.mine_ref, ...), custom_call_target="tpu_custom_call" | custom-call | flops 1000000000 | bytes 2000000 | tf_op jit(solution)/shard_map/attention/pallas_call | solution.py:484
  106.7 8.4 %all_to_all.37.context_ref = bf16[4,64,256]{2,1,0:T(8,128)(2,1)S(1)} all-to-all(bf16[4,64,256]{2,1,0:T(8,128)(2,1)S(1)} %attention.1), channel_id=1, replica_groups=mesh['dp'=8,'seq'=4] {'seq'}, dimensions={0} | all-to-all | bytes 262144 | tf_op jit(solution)/shard_map/all_to_all | solution.py:505
  115.2 0.0 collective-permute-done.2.other_ref
  115.2 1.9 %output.1 = bf16[64,1024]{1,0:T(8,128)(2,1)} custom-call(s32[8]{0:T(128)S(1)} %copy-done.6, s32[8]{0:T(128)S(1)} %copy-done.7, s32[8]{0:T(128)S(1)} %copy-done.8, bf16[4,64,256]{2,1,0:T(8,128)(2,1)S(1)} %all_to_all.37.context_ref, s32[64,1]{1,0:T(8,128)S(1)} %copy-done.3, bf16[4,1024,128]{2,1,0:T(8,128)(2,1)S(1)} %all-to-all-done.6.mine_ref, ...), custom_call_target="tpu_custom_call" | custom-call | flops 100000000 | bytes 3000000 | tf_op jit(solution)/shard_map/output/pallas_call | solution.py:507
  (13 shorter events, 0.0 us)
Async XLA Ops:
  1.3 1.3 %copy-start = (bf16[640,1024]{1,0:T(8,128)(2,1)S(1)}, bf16[640,1024]{1,0:T(8,128)(2,1)}, u32[]{:S(2)}) copy-start(bf16[640,1024]{1,0:T(8,128)(2,1)} %proj_ref.1) | copy-start | bytes 3932164
  2.7 1.1 copy-start.1
  3.8 1.0 copy-start.2
  6.2 0.9 copy-start.9
  7.1 3.8 %copy-start.5 = (f32[8,5120]{1,0:T(8,128)S(1)}, f32[8,5120]{1,0:T(8,128)}, u32[]{:S(2)}) copy-start(f32[8,5120]{1,0:T(8,128)} %audio_ref.1) | copy-start | bytes 491524
  7.1 8.8 %copy-start.6 = (s32[8]{0:T(128)S(1)}, s32[8]{0:T(128)}, u32[]{:S(2)}) copy-start(s32[8]{0:T(128)} %slots_ref.5) | copy-start | bytes 100
  7.1 10.3 %copy-start.10 = (f32[512,512]{1,0:T(8,128)S(1)}, f32[512,512]{1,0:T(8,128)}, u32[]{:S(2)}) copy-start(f32[512,512]{1,0:T(8,128)} %constant.20.clone.table_ref) | copy-start | bytes 3145732
  7.1 10.3 %copy-start.11 = (bf16[640,512]{1,0:T(8,128)(2,1)S(1)}, bf16[640,512]{1,0:T(8,128)(2,1)}, u32[]{:S(2)}) copy-start(bf16[640,512]{1,0:T(8,128)(2,1)} %constant.22.clone.select_ref) | copy-start | bytes 1966084
  7.1 10.3 %copy-start.12 = (f32[256,128]{1,0:T(8,128)S(1)}, f32[256,128]{1,0:T(8,128)}, u32[]{:S(2)}) copy-start(f32[256,128]{1,0:T(8,128)} %constant.21.clone.filter_ref) | copy-start | bytes 393220
  7.1 12.5 %all-to-all-start.1 = ((bf16[2,640,512]{2,1,0:T(8,128)(2,1)}), bf16[2,640,512]{2,1,0:T(8,128)(2,1)S(1)}, u32[]{:S(2)}, u32[]{:S(2)}) async-start(bf16[2,640,512]{2,1,0:T(8,128)(2,1)} %get-tuple-element.10), calls=%async_computation.1 | async-start | bytes 2621440 | tf_op jit(solution)/shard_map/all_to_all | solution.py:394
  10.9 6.5 %collective-permute-start = (f32[8,1024]{1,0:T(8,128)S(1)}, f32[8,1024]{1,0:T(8,128)S(1)}, u32[]{:S(2)}, u32[]{:S(2)}) collective-permute-start(f32[8,1024]{1,0:T(8,128)S(1)} %slice.3), channel_id=1, source_target_pairs={{0,1},{1,2},{2,3},{3,4},{4,5},{5,6},{6,7},{7,8},{8,9},{9,10},{10,1... | collective-permute-start | bytes 98312 | tf_op jit(solution)/shard_map/ppermute | solution.py:371
  19.6 12.3 %copy-start.14 = (bf16[2,640,512]{2,1,0:T(8,128)(2,1)}, bf16[2,640,512]{2,1,0:T(8,128)(2,1)S(1)}, u32[]{:S(2)}) copy-start(bf16[2,640,512]{2,1,0:T(8,128)(2,1)S(1)} %all-to-all-done.1.proj_ref) | copy-start | bytes 3932164
  40.4 27.2 %copy-start.15 = (bf16[1024,128]{1,0:T(8,128)(2,1)S(1)}, bf16[1024,128]{1,0:T(8,128)(2,1)}, u32[]{:S(2)}) copy-start(bf16[1024,128]{1,0:T(8,128)(2,1)} %param.25) | copy-start | bytes 786436
  53.7 13.9 %all-to-all-start.4 = ((bf16[4,128,768]{2,1,0:T(8,128)(2,1)}), bf16[4,128,768]{2,1,0:T(8,128)(2,1)S(1)}, u32[]{:S(2)}, u32[]{:S(2)}) async-start(bf16[4,128,768]{2,1,0:T(8,128)(2,1)} %get-tuple-element.14), calls=%async_computation.4 | async-start | bytes 1572864 | tf_op jit(solution)/shard_map/all_to_all | solution.py:397
  68.8 3.8 %copy-start.3 = (s32[64,1]{1,0:T(8,128)S(1)}, s32[64,1]{1,0:T(8,128)}, u32[]{:S(2)}) copy-start(s32[64,1]{1,0:T(8,128)} %constant.24.clone.sample_ref) | copy-start | bytes 772
  68.8 3.8 %copy-start.4 = (bf16[64,64]{1,0:T(8,128)(2,1)S(1)}, bf16[64,64]{1,0:T(8,128)(2,1)}, u32[]{:S(2)}) copy-start(bf16[64,64]{1,0:T(8,128)(2,1)} %constant.23.clone.swap_ref.frames_ref) | copy-start | bytes 24580
  68.8 3.8 %copy-start.7 = (s32[8]{0:T(128)S(1)}, s32[8]{0:T(128)}, u32[]{:S(2)}) copy-start(s32[8]{0:T(128)} %starts_ref.5) | copy-start | bytes 100
  68.8 3.8 %copy-start.8 = (s32[8]{0:T(128)S(1)}, s32[8]{0:T(128)}, u32[]{:S(2)}) copy-start(s32[8]{0:T(128)} %lengths_ref.5) | copy-start | bytes 100
  68.8 16.7 %all-to-all-start.6 = ((bf16[4,1024,128]{2,1,0:T(8,128)(2,1)}), bf16[4,1024,128]{2,1,0:T(8,128)(2,1)S(1)}, u32[]{:S(2)}, u32[]{:S(2)}) async-start(bf16[4,1024,128]{2,1,0:T(8,128)(2,1)} %broadcast_in_dim.2), calls=%async_computation.6 | async-start | bytes 2097152 | tf_op jit(solution)/shard_map/all_to_all | solution.py:474
  72.5 30.4 %copy-start.13 = (s32[1,256]{1,0:T(1,128)S(1)}, s32[1,256]{1,0:T(1,128)}, u32[]{:S(2)}) copy-start(s32[1,256]{1,0:T(1,128)} %constant.25.clone.sample_ref) | copy-start | bytes 3076
  72.5 16.6 %collective-permute-start.1 = (bf16[4,128,768]{2,1,0:T(8,128)(2,1)S(1)}, bf16[4,128,768]{2,1,0:T(8,128)(2,1)}, u32[]{:S(2)}, u32[]{:S(2)}) collective-permute-start(bf16[4,128,768]{2,1,0:T(8,128)(2,1)S(1)} %all-to-all-done.4.mine_ref), channel_id=1, source_target_pairs={{0,4},{4,0},{8,12},{12,8},{16,20},{20,16},{24,28},{28,24},{1,5},{5... | collective-permute-start | bytes 2359304 | tf_op jit(solution)/shard_map/ppermute | solution.py:400
  85.5 17.4 %all-to-all-start.3 = ((bf16[4,64,1024]{2,1,0:T(8,128)(2,1)}), bf16[4,64,1024]{2,1,0:T(8,128)(2,1)S(1)}, u32[]{:S(2)}, u32[]{:S(2)}) async-start(bf16[4,64,1024]{2,1,0:T(8,128)(2,1)} %get-tuple-element.13), calls=%async_computation.3 | async-start | bytes 1048576 | tf_op jit(solution)/shard_map/all_to_all | solution.py:472
  89.0 26.2 %collective-permute-start.2 = (bf16[4,1024,128]{2,1,0:T(8,128)(2,1)S(1)}, bf16[4,1024,128]{2,1,0:T(8,128)(2,1)S(1)}, u32[]{:S(2)}, u32[]{:S(2)}) collective-permute-start(bf16[4,1024,128]{2,1,0:T(8,128)(2,1)S(1)} %all-to-all-done.6.mine_ref), channel_id=1, source_target_pairs={{0,4},{4,0},{8,12},{12,8},{16,20},{20,16},{24,28},{28,24},{1,5},{5... | collective-permute-start | bytes 3145736 | tf_op jit(solution)/shard_map/ppermute | solution.py:482
